TPU v7x, 32 devices: a whole 2x2x4 slice. The times are simulated.
32 devices in a mesh: lat: 8 (over z, core), lon: 4 (over y, x).
Axes of the slice: x: 2, y: 2, z: 4, core: 2. Of those that a mesh axis runs over, the one named last changes fastest.
Arguments:
- east_wind: float32 [4, 4096, 8192], P(None, 'lat', 'lon'), may hold values from -6 to 6
- north_wind: float32 [4, 4096, 8192], P(None, 'lat', 'lon'), may hold values from -6 to 6
- pressure: float32 [4, 4096, 8192], P(None, 'lat', 'lon'), may hold values from -6 to 6
- sound_squared: float32 [4], replicated, may hold values from 0.5 to 2
- column_mass: float32 [4096, 8192], P('lat', 'lon'), may hold values from 0.5 to 1.5
- polar_rows: int32 [512], replicated, may hold values from 0 to 4095, as said below
- cutoffs: int32 [512], replicated, may hold values from 512 to 4095
Outputs:
- new_east: float32 [4, 4096, 8192], P(None, 'lat', 'lon')
- new_north: float32 [4, 4096, 8192], P(None, 'lat', 'lon')
- new_pressure: float32 [4, 4096, 8192], P(None, 'lat', 'lon')
Inputs may be any that keep to these rules, and one draw needn't show every extreme that they name: `polar_rows`: distinct rows in ascending order, each poleward of 45 degrees (below 1024 or at least 3072); at most 256 of them lie in one band of 512 rows (rows b * 512 to (b + 1) * 512 - 1), and some band holds exactly 256.
All inputs are finite; a program needn't handle non-finite values.
Results may differ from a plain program's by a relative error of at most 0.00005.
Values sent between devices are 32-bit elements; how exact they have to be, the bound alone decides.
A program may use at most 320 MiB of HBM per device.

v0:
```python
import jax
import jax.numpy as jnp
from jax import lax
from jax.sharding import PartitionSpec as P

PRECISE = lax.Precision.HIGHEST


def extended(shard, sides, width):
    for axis, dim in sides:
        peers, length = (lax.axis_size(axis), shard.shape[dim])
        up = [(i, (i + 1) % peers) for i in range(peers)]
        down = [(j, i) for i, j in up]
        last = lax.slice_in_dim(shard, length - width, length, axis=dim)
        first = lax.slice_in_dim(shard, 0, width, axis=dim)
        before = lax.ppermute(last, axis, up)
        after = lax.ppermute(first, axis, down)
        shard = jnp.concatenate([before, shard, after], axis=dim)
    return shard


def latitude_terms(global_rows, total_rows):
    latitude = (-0.5 + (global_rows.astype(jnp.float32) + 0.5) / total_rows) * jnp.pi
    cosine = jnp.cos(latitude)
    courant = 0.3 * jnp.minimum(1.0 / cosine, 2.0)
    return (cosine, courant)


def pole_rims(padded, band_number, band_count, lat_dim):
    extent = padded.shape[lat_dim]
    places = jnp.arange(extent)
    keeping = ((places > 0) | (band_number > 0)) & (
        (places < extent - 1) | (band_number < band_count - 1)
    )
    layout = [1] * padded.ndim
    layout[lat_dim] = extent
    return padded * keeping.astype(jnp.float32).reshape(layout)


def slot_table(polar_rows, cutoffs, band_number, row_count, slot_count):
    lower = band_number * row_count
    opening = jnp.sum((polar_rows < lower).astype(jnp.int32))
    closing = jnp.sum((polar_rows < lower + row_count).astype(jnp.int32))
    entries = opening + jnp.arange(slot_count, dtype=jnp.int32)
    present = entries < closing
    safe_entries = jnp.clip(entries, 0, polar_rows.shape[0] - 1)
    local_rows = jnp.clip(jnp.take(polar_rows, safe_entries) - lower, 0, row_count - 1)
    limits = jnp.take(cutoffs, safe_entries)
    return (present, local_rows, limits)


def dft_filter(row_data, limits):
    row_total, length = row_data.shape
    inner = 128
    outer = length // inner
    outer_ids = jnp.arange(outer, dtype=jnp.int32)
    inner_ids = jnp.arange(inner, dtype=jnp.int32)
    angle_one = (
        2.0 * jnp.pi * (outer_ids[:, None] * outer_ids[None, :] % outer).astype(jnp.float32) / outer
    )
    angle_two = (
        2.0 * jnp.pi * (inner_ids[:, None] * inner_ids[None, :] % inner).astype(jnp.float32) / inner
    )
    angle_twist = (
        2.0
        * jnp.pi
        * (outer_ids[:, None] * inner_ids[None, :] % length).astype(jnp.float32)
        / length
    )
    cos_one, sin_one = (jnp.cos(angle_one), jnp.sin(angle_one))
    cos_two, sin_two = (jnp.cos(angle_two), jnp.sin(angle_two))
    cos_twist, sin_twist = (jnp.cos(angle_twist), jnp.sin(angle_twist))
    folded = row_data.reshape(row_total, outer, inner)
    real_a = jnp.einsum("mab,ak->mkb", folded, cos_one, precision=PRECISE)
    imag_a = -jnp.einsum("mab,ak->mkb", folded, sin_one, precision=PRECISE)
    real_b = real_a * cos_twist + imag_a * sin_twist
    imag_b = imag_a * cos_twist - real_a * sin_twist
    real_c = jnp.einsum("mkb,bj->mkj", real_b, cos_two, precision=PRECISE) + jnp.einsum(
        "mkb,bj->mkj", imag_b, sin_two, precision=PRECISE
    )
    imag_c = jnp.einsum("mkb,bj->mkj", imag_b, cos_two, precision=PRECISE) - jnp.einsum(
        "mkb,bj->mkj", real_b, sin_two, precision=PRECISE
    )
    wave_ids = outer_ids[:, None] + outer * inner_ids[None, :]
    wave_ids = jnp.minimum(wave_ids, length - wave_ids)
    keeping = (wave_ids[None] <= limits[:, None, None]).astype(jnp.float32)
    real_c = real_c * keeping
    imag_c = imag_c * keeping
    real_d = jnp.einsum("mkj,jb->mkb", real_c, cos_two, precision=PRECISE) - jnp.einsum(
        "mkj,jb->mkb", imag_c, sin_two, precision=PRECISE
    )
    imag_d = jnp.einsum("mkj,jb->mkb", imag_c, cos_two, precision=PRECISE) + jnp.einsum(
        "mkj,jb->mkb", real_c, sin_two, precision=PRECISE
    )
    real_e = real_d * cos_twist - imag_d * sin_twist
    imag_e = imag_d * cos_twist + real_d * sin_twist
    result = jnp.einsum("mkb,ka->mab", real_e, cos_one, precision=PRECISE) - jnp.einsum(
        "mkb,ka->mab", imag_e, sin_one, precision=PRECISE
    )
    return (result / length).reshape(row_total, length)


def filter_round(slots, slot_limits):
    slot_total, pair_count, level_count, seg_width = slots.shape
    per_slot = pair_count * level_count
    items = slots.reshape(slot_total * per_slot, seg_width)
    whole_rows = lax.all_to_all(items, "lon", split_axis=0, concat_axis=1, tiled=True)
    share = whole_rows.shape[0]
    item_ids = lax.axis_index("lon") * share + jnp.arange(share, dtype=jnp.int32)
    item_limits = jnp.take(slot_limits, item_ids // per_slot)
    filtered = dft_filter(whole_rows, item_limits)
    returned = lax.all_to_all(filtered, "lon", split_axis=1, concat_axis=0, tiled=True)
    return returned.reshape(slot_total, pair_count, level_count, seg_width)


def on_device(east_wind, north_wind, pressure, sound_squared, column_mass, polar_rows, cutoffs):
    level_count, row_count, seg_width = pressure.shape
    band_count = lax.axis_size("lat")
    band_number = lax.axis_index("lat")
    total_rows = row_count * band_count
    global_rows = band_number * row_count + jnp.arange(row_count, dtype=jnp.int32)
    cosine, courant = latitude_terms(global_rows, total_rows)
    lat_factor = courant[None, :, None]
    padded = extended(pressure, (("lat", 1), ("lon", 2)), 1)
    padded = pole_rims(padded, band_number, band_count, 1)
    east = padded[:, 1:-1, 2:]
    west = padded[:, 1:-1, :-2]
    north = padded[:, 2:, 1:-1]
    south = padded[:, :-2, 1:-1]
    east_step = east_wind - lat_factor * (east - west) * 0.5
    north_step = north_wind - 0.3 * (north - south) * 0.5
    stacked = jnp.stack([east_step, north_step])
    slot_count = row_count // 2
    present, local_rows, limits = slot_table(
        polar_rows, cutoffs, band_number, row_count, slot_count
    )
    present_float = present.astype(jnp.float32)
    picked = jnp.moveaxis(jnp.take(stacked, local_rows, axis=2), 2, 0)
    picked = picked * present_float[:, None, None, None]
    whole_limit = seg_width * lax.axis_size("lon") // 2
    smoothed = filter_round(picked, jnp.where(present, limits, whole_limit))
    smoothed = smoothed * present_float[:, None, None, None]
    targets = jnp.where(present, local_rows, row_count)
    updated = stacked.at[:, :, targets, :].set(jnp.moveaxis(smoothed, 0, 2), mode="drop")
    new_east = updated[0]
    new_north = updated[1]
    moving = jnp.stack([new_east, new_north * cosine[None, :, None]])
    rimmed = extended(moving, (("lat", 2), ("lon", 3)), 1)
    rimmed = pole_rims(rimmed, band_number, band_count, 2)
    east_u = rimmed[0, :, 1:-1, 2:]
    west_u = rimmed[0, :, 1:-1, :-2]
    north_v = rimmed[1, :, 2:, 1:-1]
    south_v = rimmed[1, :, :-2, 1:-1]
    divergence = (
        lat_factor * (east_u - west_u) * 0.5
        + 0.3 * (north_v - south_v) * 0.5 / cosine[None, :, None]
    )
    new_pressure = pressure - sound_squared[:, None, None] * divergence / column_mass[None]
    return (new_east, new_north, new_pressure)


def solution(mesh):
    in_specs = (
        P(None, "lat", "lon"),
        P(None, "lat", "lon"),
        P(None, "lat", "lon"),
        P(),
        P("lat", "lon"),
        P(),
        P(),
    )
    out_specs = (P(None, "lat", "lon"), P(None, "lat", "lon"), P(None, "lat", "lon"))
    return jax.shard_map(
        on_device, mesh=mesh, in_specs=in_specs, out_specs=out_specs, check_vma=False
    )
```

profile of v0, /device:TPU:0, one launch (start us, length us, event | category | flops | bytes accessed | tf_op | source)
XLA Modules:
  0.0 1361.5 jit_solution(3765692962061580794)
XLA Ops:
  12.3 20.5 %constant_dynamic-update-slice_fusion.1 = f32[4,514,2048]{2,0,1:T(4,128)S(1)} fusion(f32[4,514,2048]{2,0,1:T(4,128)S(1)} %constant_dynamic-update-slice_fusion.2, f32[4,512,2048]{2,1,0:T(8,128)} %param.11), kind=kLoop, calls=%fused_computation.107 | loop fusion | bytes 33554432
  47.1 33.0 %concatenate.13 = f32[4,514,2050]{2,0,1:T(4,128)} concatenate(f32[4,514,1]{2,0,1:T(4,128)S(1)} %copy.49, f32[4,514,2048]{2,0,1:T(4,128)} %copy-done.4, f32[4,514,1]{2,0,1:T(4,128)S(1)} %copy.50), dimensions={2} | concatenate | bytes 33718400 | tf_op jit(solution)/shard_map/concatenate | solution.py:18
  97.4 52.7 %fusion.11 = (f32[1,4,512,2048]{3,1,2,0:T(4,128)}, f32[1,4,512,2048]{3,1,2,0:T(4,128)}) fusion(f32[4,514,2050]{2,0,1:T(4,128)} %broadcast_multiply_fusion.1, f32[4,512,2048]{2,1,0:T(8,128)} %param.9, f32[512]{0:T(512)S(1)} %get-tuple-element.35, f32[4,512,2048]{2,1,0:T(8,128)} %param.10), kind=kLoop, calls=%fused_computation.27 | loop fusion | flops 29360128 | bytes 134219776 | tf_op jit(solution)/shard_map/stack | solution.py:132
  150.1 23.3 %pad_maximum_fusion.1 = f32[2,4,512,2048]{3,1,2,0:T(4,128)} fusion(f32[1,4,512,2048]{3,1,2,0:T(4,128)} %get-tuple-element.30, f32[1,4,512,2048]{3,1,2,0:T(4,128)} %get-tuple-element.29), kind=kLoop, calls=%fused_computation.6 | loop fusion | flops 8388608 | bytes 67108864 | tf_op jit(solution)/shard_map/stack | solution.py:132
  207.4 19.3 %all_to_all.24 = f32[4,512,2048]{2,1,0:T(8,128)} reshape(f32[256,2,4,2048]{3,2,1,0:T(4,128)} %select_multiply_fusion) | data formatting | bytes 33554432 | tf_op jit(solution)/shard_map/all_to_all | solution.py:107
  241.6 175.0 %all-to-all-done = f32[4,512,2048]{2,1,0:T(8,128)} async-done(((f32[4,512,2048]{2,1,0:T(8,128)}), f32[4,512,2048]{2,1,0:T(8,128)}, u32[]{:S(2)}, u32[]{:S(2)}) %all-to-all-start) | async-done | bytes 16777248 | tf_op jit(solution)/shard_map/all_to_all | solution.py:107
  416.6 20.9 %copy.53 = f32[512,4,2048]{2,1,0:T(4,128)} copy(f32[512,4,2048]{2,0,1:T(8,128)} %bitcast.4) | data formatting | bytes 33554432 | tf_op jit(solution)/shard_map/all_to_all | solution.py:107
  437.5 20.6 %reshape.240 = f32[512,64,128]{2,1,0:T(8,128)} reshape(f32[512,4,2048]{2,1,0:T(4,128)} %copy.53) | data formatting | bytes 33554432 | tf_op jit(solution)/shard_map/reshape | solution.py:73
  458.1 21.9 %fusion.53 = f32[64,512,128]{2,0,1:T(8,128)} fusion(f32[512,64,128]{2,1,0:T(8,128)} %reshape.240), kind=kOutput, calls=%fused_computation.87 | convolution fusion | flops 3221282816 | bytes 33554432 | tf_op jit(solution)/shard_map/mab,ak->mkb/dot_general | solution.py:75
  480.0 31.5 %add_bitcast_fusion = (f32[512,64,128]{2,1,0:T(8,128)}, f32[512,64,128]{2,1,0:T(8,128)}) fusion(f32[64,512,128]{2,0,1:T(8,128)} %fusion.53, f32[64,128]{1,0:T(8,128)S(1)} %get-tuple-element.40, f32[64,128]{1,0:T(8,128)S(1)} %get-tuple-element.41, f32[512,64,128]{2,1,0:T(8,128)} %reshape.240), kind=kOutput, calls=%fused_computation.37 | convolution fusion | flops 3250642944 | bytes 67174400 | tf_op jit(solution)/shard_map/mab,ak->mkb/dot_general | solution.py:74
  511.5 32.6 %fusion.16 = f32[512,64,128]{2,0,1:T(8,128)} fusion(f32[512,64,128]{2,1,0:T(8,128)} %get-tuple-element.22), kind=kOutput, calls=%fused_computation.38 | convolution fusion | flops 6442680320 | bytes 33554432 | tf_op jit(solution)/shard_map/mkb,bj->mkj/dot_general | solution.py:81
  544.2 30.2 %fusion.18 = f32[512,64,128]{2,0,1:T(8,128)} fusion(f32[512,64,128]{2,1,0:T(8,128)S(1)} %copy-done.2), kind=kOutput, calls=%fused_computation.40 | convolution fusion | flops 6442680320 | bytes 33554432 | tf_op jit(solution)/shard_map/mkb,bj->mkj/dot_general | solution.py:78
  574.4 32.1 %compare_select_fusion = f32[512,64,128]{2,0,1:T(8,128)S(1)} fusion(f32[512,64,128]{2,0,1:T(8,128)} %fusion.16, f32[512,64,128]{2,1,0:T(8,128)} %get-tuple-element.21, s32[64,128]{1,0:T(8,128)S(1)} %subtract_minimum_fusion, s32[512]{0:T(512)S(1)} %and_select_fusion.1), kind=kOutput, calls=%fused_computation.7 | convolution fusion | flops 6455263232 | bytes 50366464 | tf_op jit(solution)/shard_map/mkb,bj->mkj/dot_general | solution.py:81
  606.5 33.5 %compare_select_fusion.1 = f32[512,64,128]{2,0,1:T(8,128)} fusion(f32[512,64,128]{2,0,1:T(8,128)} %fusion.18, f32[512,64,128]{2,1,0:T(8,128)} %get-tuple-element.21, s32[64,128]{1,0:T(8,128)S(1)} %subtract_minimum_fusion, s32[512]{0:T(512)S(1)} %and_select_fusion.1), kind=kOutput, calls=%fused_computation.8 | convolution fusion | flops 6455263232 | bytes 50366464 | tf_op jit(solution)/shard_map/mkb,bj->mkj/dot_general | solution.py:78
  694.7 31.1 %multiply_subtract_fusion = (f32[512,64,128]{2,0,1:T(8,128)}, f32[512,64,128]{2,0,1:T(8,128)}) fusion(f32[512,64,128]{2,0,1:T(8,128)} %convolution_subtract_fusion, f32[64,128]{1,0:T(8,128)S(1)} %get-tuple-element.40, f32[64,128]{1,0:T(8,128)S(1)} %get-tuple-element.41, f32[512,64,128]{2,0,1:T(8,128)} %fusion.37, f32[512,64,128]{2,0,1:T(8,128)} %compare_select_fusion.1), kind=kOutput, calls=%fused_computation.35 | convolution fusion | flops 6472040448 | bytes 83951616 | tf_op jit(solution)/shard_map/mkj,jb->mkb/dot_general | solution.py:92
  725.8 33.5 %fusion.12 = f32[64,512,128]{2,0,1:T(8,128)} fusion(f32[512,64,128]{2,0,1:T(8,128)} %get-tuple-element.20), kind=kOutput, calls=%fused_computation.28 | convolution fusion | flops 3221282816 | bytes 33554432 | tf_op jit(solution)/shard_map/mkb,ka->mab/dot_general | solution.py:97
  759.2 36.9 %multiply_bitcast_fusion = f32[512,64,128]{2,1,0:T(8,128)} fusion(f32[64,512,128]{2,0,1:T(8,128)} %fusion.12, f32[512,64,128]{2,0,1:T(8,128)} %get-tuple-element.19), kind=kOutput, calls=%fused_computation.33 | convolution fusion | flops 3229671424 | bytes 50331648 | tf_op jit(solution)/shard_map/mkb,ka->mab/dot_general | solution.py:97
  830.6 188.0 %all_to_all.32 = f32[512,4,2048]{2,0,1:T(8,128)} all-to-all(f32[512,4,2048]{2,0,1:T(8,128)S(1)} %copy.60), channel_id=1, replica_groups=mesh['lat'=8,'lon'=4] {'lon'}, dimensions={1} | all-to-all | bytes 33554432 | tf_op jit(solution)/shard_map/all_to_all | solution.py:112
  1053.6 46.9 %scatter_fusion = f32[2,4,512,2048]{3,1,2,0:T(4,128)} fusion(f32[2,4,512,2048]{3,1,2,0:T(4,128)} %pad_maximum_fusion.1, s32[256]{0:T(256)S(1)} %copy-done.13, f32[256,2,4,2048]{3,2,1,0:T(4,128)} %broadcast_multiply_fusion.2), kind=kCustom, calls=%fused_computation.4 | custom fusion | bytes 50332672 | tf_op jit(solution)/shard_map/scatter | solution.py:144
  1100.5 31.1 %fusion.141 = (f32[1,4,512,2048]{3,1,2,0:T(4,128)S(1)}, f32[4,512,2048]{2,0,1:T(4,128)}, f32[1,4,512,2048]{3,1,2,0:T(4,128)}, f32[4,512,2048]{2,0,1:T(4,128)}) fusion(f32[2,4,512,2048]{3,1,2,0:T(4,128)} %scatter_fusion, f32[512]{0:T(512)S(1)} %copy-done.10), kind=kLoop, calls=%fused_computation.198 | loop fusion | flops 4194304 | bytes 100665344 | tf_op jit(solution)/shard_map/slice | solution.py:145
  1143.3 23.4 %pad_maximum_fusion = f32[2,4,514,2048]{3,1,2,0:T(4,128)} fusion(f32[2,4,1,2048]{3,1,2,0:T(4,128)S(1)} %collective-permute-done.5, f32[1,4,512,2048]{3,1,2,0:T(4,128)} %get-tuple-element.27, f32[1,4,512,2048]{3,1,2,0:T(4,128)} %copy-done.3, f32[2,4,1,2048]{3,1,2,0:T(4,128)S(1)} %collective-permute-done.4), kind=kLoop, calls=%fused_computation.5 | loop fusion | flops 25264128 | bytes 67371008 | tf_op jit(solution)/shard_map/concatenate | solution.py:18
  1215.4 64.8 %concatenate.15 = f32[2,4,514,2050]{3,1,2,0:T(4,128)} concatenate(f32[2,4,514,1]{3,1,2,0:T(4,128)} %copy.63, f32[2,4,514,2048]{3,1,2,0:T(4,128)} %pad_maximum_fusion, f32[2,4,514,1]{3,1,2,0:T(4,128)S(1)} %copy.64), dimensions={3} | concatenate | bytes 67436800 | tf_op jit(solution)/shard_map/concatenate | solution.py:18
  1280.2 24.4 %broadcast_multiply_fusion = f32[2,4,514,2050]{3,1,2,0:T(4,128)} fusion(f32[2,4,514,2050]{3,1,2,0:T(4,128)} %concatenate.15, f32[514]{0:T(1024)S(1)} %copy-done.7), kind=kLoop, calls=%fused_computation.9 | loop fusion | flops 8429600 | bytes 67438856 | tf_op jit(solution)/shard_map/mul | solution.py:37
  1305.5 36.9 %divide_subtract_fusion = f32[4,512,2048]{2,0,1:T(4,128)S(1)} fusion(f32[2,4,514,2050]{3,1,2,0:T(4,128)} %broadcast_multiply_fusion, f32[512,2048]{1,0:T(8,128)S(1)} %copy-done.5, f32[512]{0:T(512)S(1)} %copy-done.10, f32[4]{0:T(128)S(1)} %copy-done.14, f32[512]{0:T(512)S(1)} %copy-done.9, f32[4,512,2048]{2,1,0:T(8,128)} %param.11), kind=kLoop, calls=%fused_computation.10 | loop fusion | flops 41943040 | bytes 104861712 | tf_op jit(solution)/shard_map/sub | solution.py:158
  (93 shorter events, 296.1 us)
Async XLA Ops:
  0.6 233.4 %copy-start = (s32[512]{0:T(512)S(1)}, s32[512]{0:T(512)}, u32[]{:S(2)}) copy-start(s32[512]{0:T(512)} %param.15) | copy-start | bytes 6148
  1.8 10.5 collective-permute-start
  2.3 30.6 %collective-permute-start.1 = (f32[4,1,2048]{2,0,1:T(4,128)S(1)}, f32[4,1,2048]{2,0,1:T(4,128)S(1)}, u32[]{:S(2)}, u32[]{:S(2)}) collective-permute-start(f32[4,1,2048]{2,0,1:T(4,128)S(1)} %copy.92), channel_id=1, source_target_pairs={{4,0},{8,4},{12,8},{16,12},{20,16},{24,20},{28,24},{0,28},{5,1},{9... | collective-permute-start | bytes 98312 | tf_op jit(solution)/shard_map/ppermute | solution.py:17
  7.0 90.4 %copy-start.8 = (f32[512]{0:T(512)}, f32[512]{0:T(512)S(1)}, u32[]{:S(2)}) copy-start(f32[512]{0:T(512)S(1)} %get-tuple-element.35) | copy-start | bytes 6148
  12.2 177.7 %copy-start.11 = (f32[256]{0:T(256)}, f32[256]{0:T(256)S(1)}, u32[]{:S(2)}) copy-start(f32[256]{0:T(256)S(1)} %get-tuple-element.39) | copy-start | bytes 3076
  32.9 5.8 copy-start.4
  40.3 6.3 collective-permute-start.2
  42.3 3.8 collective-permute-start.3
  43.5 36.6 %copy-start.6 = (f32[514]{0:T(1024)}, f32[514]{0:T(1024)S(1)}, u32[]{:S(2)}) copy-start(f32[514]{0:T(1024)S(1)} %fusion.84) | copy-start | bytes 6172
  226.7 189.9 %all-to-all-start = ((f32[4,512,2048]{2,1,0:T(8,128)}), f32[4,512,2048]{2,1,0:T(8,128)}, u32[]{:S(2)}, u32[]{:S(2)}) async-start(f32[4,512,2048]{2,1,0:T(8,128)} %all_to_all.24), calls=%async_computation | async-start | bytes 33554432 | tf_op jit(solution)/shard_map/all_to_all | solution.py:107
  511.5 32.6 %copy-start.2 = (f32[512,64,128]{2,1,0:T(8,128)S(1)}, f32[512,64,128]{2,1,0:T(8,128)}, u32[]{:S(2)}) copy-start(f32[512,64,128]{2,1,0:T(8,128)} %get-tuple-element.22) | copy-start | bytes 50331652
  1018.6 19.0 %copy-start.12 = (f32[256]{0:T(256)S(1)}, f32[256]{0:T(256)}, u32[]{:S(2)}) copy-start(f32[256]{0:T(256)} %copy-done.11) | copy-start | bytes 3076
  1037.5 16.1 %copy-start.13 = (s32[256]{0:T(256)S(1)}, s32[256]{0:T(256)}, u32[]{:S(2)}) copy-start(s32[256]{0:T(256)} %get-tuple-element.37) | copy-start | bytes 3076
  1053.6 46.9 %copy-start.10 = (f32[512]{0:T(512)S(1)}, f32[512]{0:T(512)}, u32[]{:S(2)}) copy-start(f32[512]{0:T(512)} %get-tuple-element.36) | copy-start | bytes 6148
  1131.6 6.2 copy-start.3
  1137.8 5.5 collective-permute-start.4
  1137.8 5.5 collective-permute-start.5
  1173.5 39.0 %collective-permute-start.7 = (f32[2,4,514,1]{2,1,3,0:T(4,128)S(1)}, f32[2,4,514,1]{2,1,3,0:T(4,128)S(1)}, u32[]{:S(2)}, u32[]{:S(2)}) collective-permute-start(f32[2,4,514,1]{2,1,3,0:T(4,128)S(1)} %copy.62), channel_id=1, source_target_pairs={{1,0},{2,1},{3,2},{0,3},{5,4},{6,5},{7,6},{4,7},{9,8},{10,9},{11,1... | collective-permute-start | bytes 49352 | tf_op jit(solution)/shard_map/ppermute | solution.py:17
  1175.8 37.8 %collective-permute-start.6 = (f32[2,4,514,1]{2,1,3,0:T(4,128)S(1)}, f32[2,4,514,1]{2,1,3,0:T(4,128)S(1)}, u32[]{:S(2)}, u32[]{:S(2)}) collective-permute-start(f32[2,4,514,1]{2,1,3,0:T(4,128)S(1)} %copy.61), channel_id=1, source_target_pairs={{0,1},{1,2},{2,3},{3,0},{4,5},{5,6},{6,7},{7,4},{8,9},{9,10},{10,1... | collective-permute-start | bytes 49352 | tf_op jit(solution)/shard_map/ppermute | solution.py:16
  1215.4 64.8 %copy-start.7 = (f32[514]{0:T(1024)S(1)}, f32[514]{0:T(1024)}, u32[]{:S(2)}) copy-start(f32[514]{0:T(1024)} %copy-done.6) | copy-start | bytes 6172
  1280.2 25.3 %copy-start.5 = (f32[512,2048]{1,0:T(8,128)S(1)}, f32[512,2048]{1,0:T(8,128)}, u32[]{:S(2)}) copy-start(f32[512,2048]{1,0:T(8,128)} %param.13) | copy-start | bytes 12582916
  1280.2 25.3 %copy-start.9 = (f32[512]{0:T(512)S(1)}, f32[512]{0:T(512)}, u32[]{:S(2)}) copy-start(f32[512]{0:T(512)} %copy-done.8) | copy-start | bytes 6148
  1280.2 25.3 %copy-start.14 = (f32[4]{0:T(128)S(1)}, f32[4]{0:T(128)}, u32[]{:S(2)}) copy-start(f32[4]{0:T(128)} %param.12) | copy-start | bytes 52
  1305.5 55.8 %copy-start.1 = (s32[512]{0:T(512)S(1)}, s32[512]{0:T(512)}, u32[]{:S(2)}) copy-start(s32[512]{0:T(512)} %param.15) | copy-start | bytes 6148
where the time goes:
time: 1370 us; the launch traced here: 1360 us
  local copies, waits for them, and re-layouts  385 us (28%)
  matrix products  338 us (25%)
  other arithmetic  249 us (18%)
  blocking collectives  188 us (14%)
  waiting for transfers between devices  180 us (13%)
  starting transfers between devices  20.8 us (2%)
    all_to_all x1, blocking collectives, filter_round(): lax.all_to_all(filtered, 'lon', split_axis=1, concat_axis=0, tiled=True)  188 us
    all_to_all x1, waiting for transfers between devices, filter_round(): lax.all_to_all(items, 'lon', split_axis=0, concat_axis=1, tiled=True)  175 us
    concatenate x3, local copies, waits for them, and re-layouts, extended(): shard = jnp.concatenate([before, shard, after], axis=dim)  97.8 us
    unnamed x37, local copies, waits for them, and re-layouts  87.4 us
    another operation x2, other arithmetic, on_device(): stacked = jnp.stack([east_step, north_step])  76 us
    scatter x1, local copies, waits for them, and re-layouts, on_device(): stacked.at[:, :, targets, :].set(jnp.moveaxis(smoothed, 0, 2), mode='drop')  46.9 us
    mul x2, other arithmetic, pole_rims(): return padded * keeping.astype(jnp.float32).reshape(layout)  41.6 us
    all_to_all x2, local copies, waits for them, and re-layouts, filter_round(): lax.all_to_all(items, 'lon', split_axis=0, concat_axis=1, tiled=True)  40.2 us
  transfers between devices with their start and end apart: 9, of which 3 were waited for; matrix products, arithmetic and copies ran while one was open for 5% of the time, Pallas kernels for 0%

commit v1 on v0

v1 whole, which is shorter than its diff:
```python
import jax
import jax.numpy as jnp
from jax import lax
from jax.sharding import PartitionSpec as P

PRECISE = lax.Precision.HIGHEST
CLOSE = lax.Precision.HIGH


def shifted(shard, axis, dim, rim_zero):
    peers, length = (lax.axis_size(axis), shard.shape[dim])
    up = [(i, (i + 1) % peers) for i in range(peers)]
    down = [(j, i) for i, j in up]
    last = lax.slice_in_dim(shard, length - 1, length, axis=dim)
    first = lax.slice_in_dim(shard, 0, 1, axis=dim)
    before = lax.ppermute(last, axis, up)
    after = lax.ppermute(first, axis, down)
    if rim_zero:
        place = lax.axis_index(axis)
        before = jnp.where(place > 0, before, 0.0)
        after = jnp.where(place < peers - 1, after, 0.0)
    above = jnp.concatenate([lax.slice_in_dim(shard, 1, length, axis=dim), after], axis=dim)
    below = jnp.concatenate([before, lax.slice_in_dim(shard, 0, length - 1, axis=dim)], axis=dim)
    return above, below


def latitude_terms(global_rows, total_rows):
    latitude = (-0.5 + (global_rows.astype(jnp.float32) + 0.5) / total_rows) * jnp.pi
    cosine = jnp.cos(latitude)
    courant = 0.3 * jnp.minimum(1.0 / cosine, 2.0)
    return (cosine, courant)


def slot_table(polar_rows, cutoffs, band_number, row_count, slot_count):
    lower = band_number * row_count
    opening = jnp.sum((polar_rows < lower).astype(jnp.int32))
    closing = jnp.sum((polar_rows < lower + row_count).astype(jnp.int32))
    entries = opening + jnp.arange(slot_count, dtype=jnp.int32)
    present = entries < closing
    safe_entries = jnp.clip(entries, 0, polar_rows.shape[0] - 1)
    local_rows = jnp.clip(jnp.take(polar_rows, safe_entries) - lower, 0, row_count - 1)
    limits = jnp.take(cutoffs, safe_entries)
    return (present, local_rows, limits)


def dft_filter(row_data, limits):
    row_total, length = row_data.shape
    inner = 128
    outer = length // inner
    outer_ids = jnp.arange(outer, dtype=jnp.int32)
    inner_ids = jnp.arange(inner, dtype=jnp.int32)
    angle_one = (
        2.0 * jnp.pi * (outer_ids[:, None] * outer_ids[None, :] % outer).astype(jnp.float32) / outer
    )
    angle_two = (
        2.0 * jnp.pi * (inner_ids[:, None] * inner_ids[None, :] % inner).astype(jnp.float32) / inner
    )
    angle_twist = (
        2.0
        * jnp.pi
        * (outer_ids[:, None] * inner_ids[None, :] % length).astype(jnp.float32)
        / length
    )
    cos_one, sin_one = (jnp.cos(angle_one), jnp.sin(angle_one))
    cos_two, sin_two = (jnp.cos(angle_two), jnp.sin(angle_two))
    cos_twist, sin_twist = (jnp.cos(angle_twist), jnp.sin(angle_twist))
    folded = row_data.reshape(row_total, outer, inner)
    real_a = jnp.einsum("mab,ak->mkb", folded, cos_one, precision=CLOSE)
    imag_a = -jnp.einsum("mab,ak->mkb", folded, sin_one, precision=CLOSE)
    real_b = real_a * cos_twist + imag_a * sin_twist
    imag_b = imag_a * cos_twist - real_a * sin_twist
    real_c = jnp.einsum("mkb,bj->mkj", real_b, cos_two, precision=CLOSE) + jnp.einsum(
        "mkb,bj->mkj", imag_b, sin_two, precision=CLOSE
    )
    imag_c = jnp.einsum("mkb,bj->mkj", imag_b, cos_two, precision=CLOSE) - jnp.einsum(
        "mkb,bj->mkj", real_b, sin_two, precision=CLOSE
    )
    wave_ids = outer_ids[:, None] + outer * inner_ids[None, :]
    wave_ids = jnp.minimum(wave_ids, length - wave_ids)
    keeping = (wave_ids[None] <= limits[:, None, None]).astype(jnp.float32)
    real_c = real_c * keeping
    imag_c = imag_c * keeping
    real_d = jnp.einsum("mkj,jb->mkb", real_c, cos_two, precision=CLOSE) - jnp.einsum(
        "mkj,jb->mkb", imag_c, sin_two, precision=CLOSE
    )
    imag_d = jnp.einsum("mkj,jb->mkb", imag_c, cos_two, precision=CLOSE) + jnp.einsum(
        "mkj,jb->mkb", real_c, sin_two, precision=CLOSE
    )
    real_e = real_d * cos_twist - imag_d * sin_twist
    imag_e = imag_d * cos_twist + real_d * sin_twist
    result = jnp.einsum("mkb,ka->mab", real_e, cos_one, precision=CLOSE) - jnp.einsum(
        "mkb,ka->mab", imag_e, sin_one, precision=CLOSE
    )
    return (result / length).reshape(row_total, length)


def filter_round(items, slot_limits):
    slot_total = slot_limits.shape[0]
    whole_rows = lax.all_to_all(items, "lon", split_axis=0, concat_axis=1, tiled=True)
    share = whole_rows.shape[0]
    item_ids = lax.axis_index("lon") * share + jnp.arange(share, dtype=jnp.int32)
    item_limits = jnp.take(slot_limits, item_ids % slot_total)
    filtered = dft_filter(whole_rows, item_limits)
    return lax.all_to_all(filtered, "lon", split_axis=1, concat_axis=0, tiled=True)


def on_device(east_wind, north_wind, pressure, sound_squared, column_mass, polar_rows, cutoffs):
    level_count, row_count, seg_width = pressure.shape
    band_count = lax.axis_size("lat")
    band_number = lax.axis_index("lat")
    total_rows = row_count * band_count
    global_rows = band_number * row_count + jnp.arange(row_count, dtype=jnp.int32)
    cosine, courant = latitude_terms(global_rows, total_rows)
    lat_factor = courant[None, :, None]
    east, west = shifted(pressure, "lon", 2, False)
    north, south = shifted(pressure, "lat", 1, True)
    east_step = east_wind - lat_factor * (east - west) * 0.5
    north_step = north_wind - 0.3 * (north - south) * 0.5
    stacked = jnp.concatenate([east_step, north_step])
    slot_count = row_count // 2
    present, local_rows, limits = slot_table(
        polar_rows, cutoffs, band_number, row_count, slot_count
    )
    rows = jnp.arange(row_count, dtype=jnp.int32)
    hits = present[:, None] & (local_rows[:, None] == rows[None, :])
    one_hot = hits.astype(jnp.float32)
    listed = jnp.any(hits, axis=0)
    picked = jnp.einsum("sr,qrc->qsc", one_hot, stacked, precision=PRECISE)
    whole_limit = seg_width * lax.axis_size("lon") // 2
    smoothed = filter_round(
        picked.reshape(-1, seg_width), jnp.where(present, limits, whole_limit)
    ).reshape(picked.shape)
    spread = jnp.einsum("sr,qsc->qrc", one_hot, smoothed, precision=PRECISE)
    updated = jnp.where(listed[None, :, None], spread, stacked)
    new_east = updated[:level_count]
    new_north = updated[level_count:]
    east_u, west_u = shifted(new_east, "lon", 2, False)
    north_v, south_v = shifted(new_north * cosine[None, :, None], "lat", 1, True)
    divergence = (
        lat_factor * (east_u - west_u) * 0.5
        + 0.3 * (north_v - south_v) * 0.5 / cosine[None, :, None]
    )
    new_pressure = pressure - sound_squared[:, None, None] * divergence / column_mass[None]
    return (new_east, new_north, new_pressure)


def solution(mesh):
    in_specs = (
        P(None, "lat", "lon"),
        P(None, "lat", "lon"),
        P(None, "lat", "lon"),
        P(),
        P("lat", "lon"),
        P(),
        P(),
    )
    out_specs = (P(None, "lat", "lon"), P(None, "lat", "lon"), P(None, "lat", "lon"))
    return jax.shard_map(
        on_device, mesh=mesh, in_specs=in_specs, out_specs=out_specs, check_vma=False
    )
```

time: 1370 us -> 1050 us (0.77)
  local copies, waits for them, and re-layouts: 385 us -> 181 us
  blocking collectives: 188 us -> 0 us
  waiting for transfers between devices: 180 us -> 359 us
  other arithmetic: 249 us -> 118 us
  matrix products: 338 us -> 354 us
    all_to_all x1 -> x0, blocking collectives: 188 us -> none  [filter_round(): lax.all_to_all(filtered, 'lon', split_axis=1, concat_axis=0, tiled=True)]
    all_to_all x0 -> x1, waiting for transfers between devices: none -> 181 us  [filter_round(): lax.all_to_all(filtered, 'lon', split_axis=1, concat_axis=0, tiled=True)]
    concatenate x3 -> x0, local copies, waits for them, and re-layouts: 97.8 us -> none  [extended(): shard = jnp.concatenate([before, shard, after], axis=dim)]
    unnamed x37 -> x30, local copies, waits for them, and re-layouts: 87.4 us -> 0.73 us
    slice x7 -> x10, local copies, waits for them, and re-layouts: 10.5 us -> 92.3 us  [the longest x4 85.7 us: shifted(): lax.slice_in_dim(shard, 0, length - 1, axis=dim)]
    another operation x2 -> x0, other arithmetic: 76 us -> none  [on_device(): stacked = jnp.stack([east_step, north_step])]
    sub x0 -> x2, other arithmetic: none -> 47.8 us  [the longest x1 23.9 us: on_device(): east_step = east_wind - lat_factor * (east - west) * 0.5]
    scatter x1 -> x0, local copies, waits for them, and re-layouts: 46.9 us -> none  [on_device(): stacked.at[:, :, targets, :].set(jnp.moveaxis(smoothed, 0, 2), mode='drop')]
  transfers between devices with their start and end apart: 9 -> 10, of which waited for: 3 -> 3; matrix products, arithmetic and copies ran while one was open for 5% -> 13% of each run, Pallas kernels for 0% -> 0%
where the time goes in v1:
time: 1050 us; the launch traced here: 1040 us
  waiting for transfers between devices  359 us (34%)
  matrix products  354 us (34%)
  local copies, waits for them, and re-layouts  181 us (17%)
  other arithmetic  118 us (11%)
  starting transfers between devices  27.7 us (3%)
    all_to_all x1, waiting for transfers between devices, filter_round(): lax.all_to_all(filtered, 'lon', split_axis=1, concat_axis=0, tiled=True)  181 us
    all_to_all x1, waiting for transfers between devices, filter_round(): lax.all_to_all(items, 'lon', split_axis=0, concat_axis=1, tiled=True)  177 us
    slice x4, local copies, waits for them, and re-layouts, shifted(): lax.slice_in_dim(shard, 0, length - 1, axis=dim)  85.7 us
    all_to_all x2, local copies, waits for them, and re-layouts, filter_round(): lax.all_to_all(filtered, 'lon', split_axis=1, concat_axis=0, tiled=True)  37.1 us
    sub x1, other arithmetic, on_device(): pressure - sound_squared[:, None, None] * divergence / column_mass[None]  37.1 us
    dot_general x1, matrix products, on_device(): spread = jnp.einsum('sr,qsc->qrc', one_hot, smoothed, precision=PRECISE)  35.1 us
    dot_general x1, matrix products, dft_filter(): jnp.einsum('mkb,bj->mkj', real_b, sin_two, precision=CLOSE)  31.3 us
    dot_general x1, matrix products, dft_filter(): jnp.einsum('mkb,bj->mkj', real_b, cos_two, precision=CLOSE)  31.3 us
  transfers between devices with their start and end apart: 10, of which 3 were waited for; matrix products, arithmetic and copies ran while one was open for 13% of the time, Pallas kernels for 0%

profile of v1, /device:TPU:0, one launch (start us, length us, event | category | flops | bytes accessed | tf_op | source)
XLA Modules:
  0.0 1040.4 jit_solution(3597969222040483649)
XLA Ops:
  11.9 25.5 %fusion.152 = (f32[4,512,2047]{2,1,0:T(8,128)}, f32[4,512,2047]{2,1,0:T(8,128)}) fusion(f32[4,512,2048]{2,1,0:T(8,128)} %param.11), kind=kLoop, calls=%fused_computation.186 | loop fusion | bytes 67076096 | tf_op jit(solution)/shard_map/slice | solution.py:23
  56.7 23.9 %fusion.3 = f32[4,512,2048]{2,1,0:T(8,128)} fusion(f32[4,512,2048]{2,1,0:T(8,128)} %param.9, f32[4,512,1]{2,1,0:T(8,128)S(1)} %copy.29, f32[4,512,2047]{2,1,0:T(8,128)} %get-tuple-element.26, f32[4,512,2047]{2,1,0:T(8,128)} %get-tuple-element.25, f32[4,512,1]{2,1,0:T(8,128)S(1)} %copy.31, f32[512]{0:T(512)S(1)} %minimum_multiply_fusion), kind=kLoop, calls=%fused_computation.11 | loop fusion | flops 25165824 | bytes 67110912 | tf_op jit(solution)/shard_map/sub | solution.py:117
  80.7 23.8 %fusion.5 = f32[4,512,2048]{2,1,0:T(8,128)} fusion(f32[4,512,2048]{2,1,0:T(8,128)} %param.10, f32[4,1,2048]{2,1,0:T(1,128)S(1)} %broadcast_select_fusion.3, f32[4,511,2048]{2,1,0:T(8,128)} %get-tuple-element.30, f32[4,511,2048]{2,1,0:T(8,128)} %get-tuple-element.29, f32[4,1,2048]{2,1,0:T(1,128)S(1)} %broadcast_select_fusion.1), kind=kLoop, calls=%fused_computation.14 | loop fusion | flops 20971520 | bytes 67108864 | tf_op jit(solution)/shard_map/sub | solution.py:118
  104.5 26.7 %fusion = f32[8,2048,256]{1,2,0:T(8,128)} fusion(f32[4,512,2048]{2,1,0:T(8,128)} %fusion.5, f32[4,512,2048]{2,1,0:T(8,128)} %fusion.3, s32[256]{0:T(256)S(1)} %get-tuple-element.31, pred[256]{0:T(512)(128)(4,1)S(1)} %get-tuple-element.9), kind=kOutput, calls=%fused_computation.5 | convolution fusion | flops 25778454528 | bytes 50332928 | tf_op jit(solution)/shard_map/sr,qrc->qsc/dot_general | solution.py:128
  142.3 176.8 %all-to-all-done = f32[4,512,2048]{2,1,0:T(8,128)} async-done(((f32[4,512,2048]{2,1,0:T(8,128)}), f32[4,512,2048]{2,1,0:T(8,128)}, u32[]{:S(2)}, u32[]{:S(2)}) %all-to-all-start) | async-done | bytes 16777248 | tf_op jit(solution)/shard_map/all_to_all | solution.py:99
  319.1 20.9 %copy.32 = f32[512,4,2048]{2,1,0:T(4,128)} copy(f32[512,4,2048]{2,0,1:T(8,128)} %bitcast.5) | data formatting | bytes 33554432 | tf_op jit(solution)/shard_map/all_to_all | solution.py:99
  340.0 20.6 %reshape.194 = f32[512,64,128]{2,1,0:T(8,128)} reshape(f32[512,4,2048]{2,1,0:T(4,128)} %copy.32) | data formatting | bytes 33554432 | tf_op jit(solution)/shard_map/reshape | solution.py:67
  375.0 28.1 %add_bitcast_fusion = (f32[512,64,128]{2,1,0:T(8,128)}, f32[512,64,128]{2,1,0:T(8,128)}) fusion(f32[64,512,128]{2,0,1:T(8,128)} %fusion.64, f32[64,128]{1,0:T(8,128)S(1)} %get-tuple-element.32, f32[64,128]{1,0:T(8,128)S(1)} %get-tuple-element.33, f32[512,64,128]{2,1,0:T(8,128)} %reshape.194), kind=kOutput, calls=%fused_computation.33 | convolution fusion | flops 1640030208 | bytes 67174400 | tf_op jit(solution)/shard_map/mab,ak->mkb/dot_general | solution.py:68
  403.2 28.6 %fusion.18 = f32[512,64,128]{2,0,1:T(8,128)} fusion(f32[512,64,128]{2,1,0:T(8,128)} %get-tuple-element.13), kind=kOutput, calls=%fused_computation.34 | convolution fusion | flops 3221454848 | bytes 33554432 | tf_op jit(solution)/shard_map/mkb,bj->mkj/dot_general | solution.py:75
  431.7 28.7 %fusion.20 = f32[512,64,128]{2,0,1:T(8,128)} fusion(f32[512,64,128]{2,1,0:T(8,128)} %get-tuple-element.13), kind=kOutput, calls=%fused_computation.36 | convolution fusion | flops 3221454848 | bytes 33554432 | tf_op jit(solution)/shard_map/mkb,bj->mkj/dot_general | solution.py:72
  460.4 31.3 %compare_select_fusion = f32[512,64,128]{2,0,1:T(8,128)} fusion(f32[512,64,128]{2,0,1:T(8,128)} %fusion.18, f32[512,64,128]{2,1,0:T(8,128)} %get-tuple-element.12, s32[64,128]{1,0:T(8,128)S(1)} %subtract_minimum_fusion, s32[512]{0:T(512)S(1)} %and_select_fusion.1), kind=kOutput, calls=%fused_computation.6 | convolution fusion | flops 3234037760 | bytes 50366464 | tf_op jit(solution)/shard_map/mkb,bj->mkj/dot_general | solution.py:75
  491.8 31.3 %compare_select_fusion.1 = f32[512,64,128]{2,0,1:T(8,128)} fusion(f32[512,64,128]{2,0,1:T(8,128)} %fusion.20, f32[512,64,128]{2,1,0:T(8,128)} %get-tuple-element.12, s32[64,128]{1,0:T(8,128)S(1)} %subtract_minimum_fusion, s32[512]{0:T(512)S(1)} %and_select_fusion.1), kind=kOutput, calls=%fused_computation.7 | convolution fusion | flops 3234037760 | bytes 50366464 | tf_op jit(solution)/shard_map/mkb,bj->mkj/dot_general | solution.py:72
  551.4 17.9 %convolution_subtract_fusion = f32[512,64,128]{2,0,1:T(8,128)} fusion(f32[512,64,128]{2,0,1:T(8,128)} %fusion.51, f32[512,64,128]{2,0,1:T(8,128)} %compare_select_fusion), kind=kOutput, calls=%fused_computation.43 | convolution fusion | flops 3225649152 | bytes 50331648 | tf_op jit(solution)/shard_map/mkj,jb->mkb/dot_general | solution.py:83
  569.3 27.7 %multiply_subtract_fusion = (f32[512,64,128]{2,0,1:T(8,128)}, f32[512,64,128]{2,0,1:T(8,128)}) fusion(f32[512,64,128]{2,0,1:T(8,128)} %convolution_subtract_fusion, f32[64,128]{1,0:T(8,128)S(1)} %get-tuple-element.32, f32[64,128]{1,0:T(8,128)S(1)} %get-tuple-element.33, f32[512,64,128]{2,0,1:T(8,128)} %fusion.48, f32[512,64,128]{2,0,1:T(8,128)} %compare_select_fusion.1), kind=kOutput, calls=%fused_computation.31 | convolution fusion | flops 3250814976 | bytes 83951616 | tf_op jit(solution)/shard_map/mkj,jb->mkb/dot_general | solution.py:86
  596.9 26.1 %fusion.14 = f32[64,512,128]{2,0,1:T(8,128)} fusion(f32[512,64,128]{2,0,1:T(8,128)} %get-tuple-element.11), kind=kOutput, calls=%fused_computation.25 | convolution fusion | flops 1610670080 | bytes 33554432 | tf_op jit(solution)/shard_map/mkb,ka->mab/dot_general | solution.py:91
  623.0 29.5 %multiply_bitcast_fusion = f32[512,64,128]{2,1,0:T(8,128)} fusion(f32[64,512,128]{2,0,1:T(8,128)} %fusion.14, f32[512,64,128]{2,0,1:T(8,128)} %get-tuple-element.10), kind=kOutput, calls=%fused_computation.29 | convolution fusion | flops 1619058688 | bytes 50331648 | tf_op jit(solution)/shard_map/mkb,ka->mab/dot_general | solution.py:91
  652.6 19.2 %all_to_all.27 = f32[512,4,2048]{2,1,0:T(4,128)} reshape(f32[512,64,128]{2,1,0:T(8,128)} %multiply_bitcast_fusion) | data formatting | bytes 33554432 | tf_op jit(solution)/shard_map/all_to_all | solution.py:104
  671.7 17.9 %copy.39 = f32[512,4,2048]{2,0,1:T(8,128)} copy(f32[512,4,2048]{2,1,0:T(4,128)} %all_to_all.27) | data formatting | bytes 33554432 | tf_op jit(solution)/shard_map/all_to_all | solution.py:104
  697.1 181.5 %all-to-all-done.1 = f32[512,4,2048]{2,0,1:T(8,128)} async-done(((f32[512,4,2048]{2,0,1:T(8,128)}), f32[512,4,2048]{2,0,1:T(8,128)}, u32[]{:S(2)}, u32[]{:S(2)}) %all-to-all-start.1) | async-done | bytes 16777248 | tf_op jit(solution)/shard_map/all_to_all | solution.py:104
  878.6 35.1 %bitcast_select_fusion = f32[8,512,2048]{2,1,0:T(8,128)} fusion(f32[4,512,2048]{2,1,0:T(8,128)} %fusion.5, f32[4,512,2048]{2,1,0:T(8,128)} %fusion.3, f32[8,256,2048]{2,1,0:T(8,128)} %bitcast.13, pred[512]{0:T(512)(128)(4,1)S(1)} %fusion.34, s32[256]{0:T(256)S(1)} %copy-done.6, pred[256]{0:T(512)(128)(4,1)S(1)} %copy-done.8), kind=kOutput, calls=%fused_computation.4 | convolution fusion | flops 25786843136 | bytes 83887872 | tf_op jit(solution)/shard_map/sr,qsc->qrc/dot_general | solution.py:133
  915.6 24.3 %fusion.148 = (f32[4,512,2047]{2,1,0:T(8,128)}, f32[4,512,2047]{2,1,0:T(8,128)}) fusion(f32[8,512,2048]{2,1,0:T(8,128)} %bitcast_select_fusion), kind=kLoop, calls=%fused_computation.182 | loop fusion | bytes 67076096 | tf_op jit(solution)/shard_map/slice | solution.py:23
  942.6 29.9 %broadcast_multiply_fusion = (f32[4,512,2048]{2,1,0:T(8,128)}, f32[4,512,2048]{2,1,0:T(8,128)}, f32[4,512,2048]{2,1,0:T(8,128)}) fusion(f32[512]{0:T(512)S(1)} %multiply_cosine_fusion, f32[8,512,2048]{2,1,0:T(8,128)} %bitcast_select_fusion), kind=kLoop, calls=%fused_computation.44 | loop fusion | flops 4194304 | bytes 83888128 | tf_op jit(solution)/shard_map/mul | solution.py:138
  973.6 24.0 %fusion.150 = (f32[4,511,2048]{2,1,0:T(8,128)}, f32[4,511,2048]{2,1,0:T(8,128)}) fusion(f32[4,512,2048]{2,1,0:T(8,128)} %get-tuple-element.6), kind=kLoop, calls=%fused_computation.184 | loop fusion | bytes 66977792 | tf_op jit(solution)/shard_map/slice | solution.py:23
  1002.9 37.1 %fusion.11 = f32[4,512,2048]{2,1,0:T(8,128)} fusion(f32[4,512,2048]{2,1,0:T(8,128)} %param.11, f32[4,512,1]{2,1,0:T(8,128)S(1)} %copy.43, f32[4,512,2047]{2,1,0:T(8,128)} %get-tuple-element.17, f32[4,512,2047]{2,1,0:T(8,128)} %get-tuple-element.16, f32[4,512,1]{2,1,0:T(8,128)S(1)} %copy.45, f32[4,1,2048]{2,1,0:T(1,128)S(1)} %broadcast_select_fusion.2, ...), kind=kLoop, calls=%fused_computation.21 | loop fusion | flops 58720256 | bytes 104861712 | tf_op jit(solution)/shard_map/sub | solution.py:143
  (83 shorter events, 102.4 us)
Async XLA Ops:
  0.6 51.9 %copy-start = (s32[512]{0:T(512)S(1)}, s32[512]{0:T(512)}, u32[]{:S(2)}) copy-start(s32[512]{0:T(512)} %param.15) | copy-start | bytes 6148
  1.7 78.9 %collective-permute-start.3 = (f32[4,1,2048]{2,1,0:T(1,128)S(1)}, f32[4,1,2048]{2,1,0:T(1,128)S(1)}, u32[]{:S(2)}, u32[]{:S(2)}) collective-permute-start(f32[4,1,2048]{2,1,0:T(1,128)S(1)} %get-tuple-element.27), channel_id=1, source_target_pairs={{0,4},{4,8},{8,12},{12,16},{16,20},{20,24},{24,28},{28,0},{1,5},{5... | collective-permute-start | bytes 98312 | tf_op jit(solution)/shard_map/ppermute | solution.py:16
  2.2 78.4 %collective-permute-start.2 = (f32[4,1,2048]{2,1,0:T(1,128)S(1)}, f32[4,1,2048]{2,1,0:T(1,128)S(1)}, u32[]{:S(2)}, u32[]{:S(2)}) collective-permute-start(f32[4,1,2048]{2,1,0:T(1,128)S(1)} %get-tuple-element.28), channel_id=1, source_target_pairs={{4,0},{8,4},{12,8},{16,12},{20,16},{24,20},{28,24},{0,28},{5,1},{9... | collective-permute-start | bytes 98312 | tf_op jit(solution)/shard_map/ppermute | solution.py:17
  8.6 47.7 %collective-permute-start = (f32[4,512,1]{1,0,2:T(4,128)S(1)}, f32[4,512,1]{1,0,2:T(4,128)S(1)}, u32[]{:S(2)}, u32[]{:S(2)}) collective-permute-start(f32[4,512,1]{1,0,2:T(4,128)S(1)} %copy.48), channel_id=1, source_target_pairs={{1,0},{2,1},{3,2},{0,3},{5,4},{6,5},{7,6},{4,7},{9,8},{10,9},{11,1... | collective-permute-start | bytes 24584 | tf_op jit(solution)/shard_map/ppermute | solution.py:17
  11.8 44.1 %collective-permute-start.1 = (f32[4,512,1]{1,0,2:T(4,128)S(1)}, f32[4,512,1]{1,0,2:T(4,128)S(1)}, u32[]{:S(2)}, u32[]{:S(2)}) collective-permute-start(f32[4,512,1]{1,0,2:T(4,128)S(1)} %copy.49), channel_id=1, source_target_pairs={{0,1},{1,2},{2,3},{3,0},{4,5},{5,6},{6,7},{7,4},{8,9},{9,10},{10,1... | collective-permute-start | bytes 24584 | tf_op jit(solution)/shard_map/ppermute | solution.py:16
  11.8 25.6 %slice-start = ((s8[16777216]{0:T(1024)(128)(4,1)}), s8[4194304]{0:T(1024)(128)(4,1)S(1)}, s32[]{:S(2)}) async-start(s8[16777216]{0:T(1024)(128)(4,1)} %bitcast.59), calls=%async_computation.2 | async-start | bytes 8388608
  11.9 25.6 %slice-start.1 = ((s8[16777216]{0:T(1024)(128)(4,1)}), s8[4194304]{0:T(1024)(128)(4,1)S(1)}, s32[]{:S(2)}) async-start(s8[16777216]{0:T(1024)(128)(4,1)} %bitcast.59), calls=%async_computation.3 | async-start | bytes 8388608
  11.9 25.6 %slice-start.2 = ((s8[16777216]{0:T(1024)(128)(4,1)}), s8[4194304]{0:T(1024)(128)(4,1)S(1)}, s32[]{:S(2)}) async-start(s8[16777216]{0:T(1024)(128)(4,1)} %bitcast.59), calls=%async_computation.4 | async-start | bytes 8388608
  11.9 25.6 %slice-start.3 = ((s8[16777216]{0:T(1024)(128)(4,1)}), s8[4194304]{0:T(1024)(128)(4,1)S(1)}, s32[]{:S(2)}) async-start(s8[16777216]{0:T(1024)(128)(4,1)} %bitcast.59), calls=%async_computation.5 | async-start | bytes 8388608
  37.5 11.9 %copy-start.2 = (s32[512]{0:T(512)S(1)}, s32[512]{0:T(512)}, u32[]{:S(2)}) copy-start(s32[512]{0:T(512)} %param.14) | copy-start | bytes 6148
  55.8 48.7 %copy-start.5 = (s32[256]{0:T(256)}, s32[256]{0:T(256)S(1)}, u32[]{:S(2)}) copy-start(s32[256]{0:T(256)S(1)} %get-tuple-element.31) | copy-start | bytes 3076
  55.8 48.7 %copy-start.7 = (pred[256]{0:T(512)(128)(4,1)}, pred[256]{0:T(512)(128)(4,1)S(1)}, u32[]{:S(2)}) copy-start(pred[256]{0:T(512)(128)(4,1)S(1)} %get-tuple-element.9) | copy-start | bytes 772
  55.9 24.7 %copy-start.3 = (f32[512]{0:T(512)}, f32[512]{0:T(512)S(1)}, u32[]{:S(2)}) copy-start(f32[512]{0:T(512)S(1)} %minimum_multiply_fusion) | copy-start | bytes 6148
  131.2 187.9 %all-to-all-start = ((f32[4,512,2048]{2,1,0:T(8,128)}), f32[4,512,2048]{2,1,0:T(8,128)}, u32[]{:S(2)}, u32[]{:S(2)}) async-start(f32[4,512,2048]{2,1,0:T(8,128)} %bitcast.61), calls=%async_computation | async-start | bytes 33554432 | tf_op jit(solution)/shard_map/all_to_all | solution.py:99
  689.7 7.3 copy-start.6
  689.7 7.3 copy-start.8
  689.7 188.9 %all-to-all-start.1 = ((f32[512,4,2048]{2,0,1:T(8,128)}), f32[512,4,2048]{2,0,1:T(8,128)}, u32[]{:S(2)}, u32[]{:S(2)}) async-start(f32[512,4,2048]{2,0,1:T(8,128)} %copy.39), calls=%async_computation.1 | async-start | bytes 33554432 | tf_op jit(solution)/shard_map/all_to_all | solution.py:104
  940.5 61.1 %collective-permute-start.4 = (f32[4,512,1]{1,0,2:T(4,128)S(1)}, f32[4,512,1]{1,0,2:T(4,128)S(1)}, u32[]{:S(2)}, u32[]{:S(2)}) collective-permute-start(f32[4,512,1]{1,0,2:T(4,128)S(1)} %copy.42), channel_id=1, source_target_pairs={{1,0},{2,1},{3,2},{0,3},{5,4},{6,5},{7,6},{4,7},{9,8},{10,9},{11,1... | collective-permute-start | bytes 24584 | tf_op jit(solution)/shard_map/ppermute | solution.py:17
  942.0 59.2 %collective-permute-start.5 = (f32[4,512,1]{1,0,2:T(4,128)S(1)}, f32[4,512,1]{1,0,2:T(4,128)S(1)}, u32[]{:S(2)}, u32[]{:S(2)}) collective-permute-start(f32[4,512,1]{1,0,2:T(4,128)S(1)} %copy.44), channel_id=1, source_target_pairs={{0,1},{1,2},{2,3},{3,0},{4,5},{5,6},{6,7},{7,4},{8,9},{9,10},{10,1... | collective-permute-start | bytes 24584 | tf_op jit(solution)/shard_map/ppermute | solution.py:16
  973.5 29.3 %copy-start.4 = (f32[512]{0:T(512)S(1)}, f32[512]{0:T(512)}, u32[]{:S(2)}) copy-start(f32[512]{0:T(512)} %copy-done.3) | copy-start | bytes 6148
  973.5 29.3 %copy-start.9 = (f32[4]{0:T(128)S(1)}, f32[4]{0:T(128)}, u32[]{:S(2)}) copy-start(f32[4]{0:T(128)} %param.12) | copy-start | bytes 52
  973.6 28.4 %collective-permute-start.7 = (f32[4,1,2048]{2,1,0:T(1,128)S(1)}, f32[4,1,2048]{2,1,0:T(1,128)S(1)}, u32[]{:S(2)}, u32[]{:S(2)}) collective-permute-start(f32[4,1,2048]{2,1,0:T(1,128)S(1)} %get-tuple-element.19), channel_id=1, source_target_pairs={{0,4},{4,8},{8,12},{12,16},{16,20},{20,24},{24,28},{28,0},{1,5},{5... | collective-permute-start | bytes 98312 | tf_op jit(solution)/shard_map/ppermute | solution.py:16
  997.7 5.1 collective-permute-start.6
  1002.8 37.1 %copy-start.1 = (s32[512]{0:T(512)S(1)}, s32[512]{0:T(512)}, u32[]{:S(2)}) copy-start(s32[512]{0:T(512)} %param.15) | copy-start | bytes 6148
